TPU v7x, 256 devices: a whole 4x4x8 slice. The times are simulated.
256 devices in a mesh: row: 32 (over x, z), col: 8 (over y, core).
Axes of the slice: x: 4, y: 4, z: 8, core: 2. Of those that a mesh axis runs over, the one named last changes fastest.
Arguments:
- features: bfloat16 [64, 32768], P(None, ('col', 'row')), may hold values from -4 to 4
- targets: float32 [128, 32768], P(None, ('col', 'row')), may hold values from -6 to 6
Outputs:
- coefficients: float32 [128, 32768], P(None, ('col', 'row'))
- residual: float32 [128, 32768], P(None, ('col', 'row'))
- direction: float32 [128, 32768], P(None, ('col', 'row'))
All inputs are finite; a program needn't handle non-finite values.
Results may differ from a plain program's by a relative error of at most 0.0061.
Values may be sent and summed in bfloat16 or wider, within the bound.
A program may use at most 64 MiB of HBM per device.

v0:
```python
import jax
import jax.numpy as jnp
from jax import lax
from jax.sharding import PartitionSpec as P

F = 64


ridge_weight = 0.5
kernel_gain = 2.0
sharpness = 3.0


def tile_term(rows_feat, rows_sq, cols_feat, cols_panel):
    cols_wide = cols_feat.astype(jnp.float32)
    cols_sq = jnp.sum(cols_wide * cols_wide, axis=0)
    total_rows = rows_feat.shape[1]
    block_size = min(512, total_rows)
    blocks = total_rows // block_size
    row_blocks = rows_feat.reshape(rows_feat.shape[0], blocks, block_size).transpose(1, 0, 2)
    sq_blocks = rows_sq.reshape(blocks, block_size)

    def block_image(operands):
        row_part, row_norms = operands
        inner = lax.dot_general(
            row_part, cols_feat, (((0,), (0,)), ((), ())), preferred_element_type=jnp.float32
        )
        distance = row_norms[:, None] + cols_sq[None, :] - 2.0 * inner
        entries = jnp.exp(-sharpness * distance / F).astype(jnp.bfloat16)
        return lax.dot_general(
            cols_panel, entries, (((1,), (1,)), ((), ())), preferred_element_type=jnp.float32
        )

    stacked = lax.map(block_image, (row_blocks, sq_blocks))
    return stacked.transpose(1, 0, 2).reshape(cols_panel.shape[0], total_rows)


def squared_norms(feat):
    wide = feat.astype(jnp.float32)
    return jnp.sum(wide * wide, axis=0)


def gram(left, right):
    return lax.dot_general(left, right, (((1,), (1,)), ((), ())), precision=lax.Precision.HIGHEST)


def cholesky_factor(matrix):
    size = matrix.shape[0]
    index = jnp.arange(size, dtype=jnp.int32)

    def step(position, state):
        rest, factor = state
        pos = jnp.asarray(position).astype(jnp.int32)
        column = lax.dynamic_slice_in_dim(rest, pos, 1, 1)[:, 0]
        pivot = jnp.sqrt(lax.dynamic_slice_in_dim(column, pos, 1, 0)[0])
        column = jnp.where(index >= pos, column / pivot, jnp.zeros_like(column))
        rest = rest - column[:, None] * column[None, :]
        factor = lax.dynamic_update_slice_in_dim(factor, column[:, None], pos, 1)
        return (rest, factor)

    return lax.fori_loop(0, size, step, (matrix, jnp.zeros_like(matrix)))[1]


def solve_with(factor, rhs):
    size = factor.shape[0]

    def forward(position, solved):
        pos = jnp.asarray(position).astype(jnp.int32)
        line = lax.dynamic_slice_in_dim(factor, pos, 1, 0)
        pivot = lax.dynamic_slice_in_dim(line[0], pos, 1, 0)[0]
        value = (
            lax.dynamic_slice_in_dim(rhs, pos, 1, 0)
            - jnp.dot(line, solved, precision=lax.Precision.HIGHEST)
        ) / pivot
        return lax.dynamic_update_slice_in_dim(solved, value, pos, 0)

    middle = lax.fori_loop(0, size, forward, jnp.zeros_like(rhs))

    def backward(step_count, solved):
        pos = (size - 1 - jnp.asarray(step_count)).astype(jnp.int32)
        line = lax.dynamic_slice_in_dim(factor, pos, 1, 1)
        pivot = lax.dynamic_slice_in_dim(line[:, 0], pos, 1, 0)[0]
        value = (
            lax.dynamic_slice_in_dim(middle, pos, 1, 0)
            - jnp.dot(line.T, solved, precision=lax.Precision.HIGHEST)
        ) / pivot
        return lax.dynamic_update_slice_in_dim(solved, value, pos, 0)

    return lax.fori_loop(0, size, backward, jnp.zeros_like(rhs))


def local(features, targets):
    panel = targets.astype(jnp.bfloat16)
    rows_feat = lax.all_gather(features, "col", axis=1, tiled=True)
    rows_sq = squared_norms(rows_feat)
    partial_image = tile_term(
        rows_feat,
        rows_sq,
        lax.all_gather(features, "row", axis=1, tiled=True),
        lax.all_gather(panel, "row", axis=1, tiled=True),
    )
    kernel_image = lax.psum_scatter(partial_image, "col", scatter_dimension=1, tiled=True)
    image = ridge_weight * targets + kernel_gain * kernel_image
    squares, curvature = lax.psum((gram(targets, targets), gram(targets, image)), ("row", "col"))
    sym = 0.5 * (curvature + curvature.T)
    factor = cholesky_factor(sym)
    step_size = solve_with(factor, squares)
    residual = targets - jnp.dot(step_size.T, image, precision=lax.Precision.HIGHEST)
    conjugacy = lax.psum(gram(image, residual), ("row", "col"))
    coefficients = jnp.dot(step_size.T, targets, precision=lax.Precision.HIGHEST)
    correction = -solve_with(factor, conjugacy)
    direction = residual + jnp.dot(correction.T, targets, precision=lax.Precision.HIGHEST)
    return (coefficients, residual, direction)


def solution(mesh):
    return jax.shard_map(
        local,
        mesh=mesh,
        in_specs=(P(None, ("col", "row")), P(None, ("col", "row"))),
        out_specs=(P(None, ("col", "row")), P(None, ("col", "row")), P(None, ("col", "row"))),
        check_vma=False,
    )
```

profile of v0, /device:TPU:1, one launch (start us, length us, event | category | flops | bytes accessed | tf_op | source)
XLA Modules:
  0.0 1720.8 jit_solution(16976305173994031126)
XLA Ops:
  8.8 14.6 all_gather.9
  23.5 41.9 %all_gather.10 = bf16[64,4096]{1,0:T(8,128)(2,1)S(1)} all-gather(bf16[64,128]{1,0:T(8,128)(2,1)} %param.14), channel_id=1, replica_groups=mesh['row'=32,'col'=8] {'row'}, dimensions={1}, use_global_device_ids=true | all-gather | bytes 540672 | tf_op jit(solution)/shard_map/all_gather | solution.py:99
  65.5 16.6 all-gather.2.cloned.1.call-done
  82.2 7.7 while.95
  82.2 3.8 fusion.65
  86.0 3.8 fusion.65
  91.7 33.0 %reduce-scatter.2.cloned.1.call-done = f32[128,128]{0,1:T(8,128)} async-done(((f32[128,1024]{0,1:T(8,128)}), f32[128,128]{0,1:T(8,128)}) %reduce-scatter.2.cloned.1.call-update) | async-done | bytes 65552 | tf_op jit(solution)/shard_map/reduce_scatter | solution.py:102
  124.7 1.8 convolution_bitcast_fusion
  126.6 247.5 %all-reduce.6.cloned.1.call-done = (f32[128,128]{1,0:T(8,128)}, f32[128,128]{0,1:T(8,128)}) async-done(((f32[128,128]{1,0:T(8,128)}, f32[128,128]{0,1:T(8,128)}), (f32[128,128]{1,0:T(8,128)}, f32[128,128]{0,1:T(8,128)})) %all-reduce.6.cloned.1.call-update) | async-done | bytes 131088 | tf_op jit(solution)/shard_map/psum | solution.py:104
  375.9 186.7 %while.100 = (s32[]{:T(128)}, f32[128,128]{0,1:T(8,128)S(1)}, f32[128,128]{0,1:T(8,128)S(1)}, s32[]{:T(128)}, s32[]{:T(128)}, /*index=5*/s32[]{:T(128)}) while((s32[]{:T(128)}, f32[128,128]{0,1:T(8,128)S(1)}, f32[128,128]{0,1:T(8,128)S(1)}, s32[]{:T(128)}, s32[]{:T(128)}, /*index=5*/s32[]{:T(128)}) %tuple.218), condition=%wide.region_7.8_spmd.clone, body=%wide.region_6.7_spmd.clone.sunk | while | flops 33411 | bytes 137329 | solution.py:61
  562.7 271.6 %while.96 = (s32[]{:T(128)}, f32[128,128]{1,0:T(8,128)S(1)}, f32[128,128]{1,0:T(8,128)}, f32[128,128]{1,0:T(8,128)S(1)}, s32[]{:T(128)}, /*index=5*/s32[]{:T(128)}, s32[]{:T(128)}) while((s32[]{:T(128)}, f32[128,128]{1,0:T(8,128)S(1)}, f32[128,128]{1,0:T(8,128)}, f32[128,128]{1,0:T(8,128)S(1)}, s32[]{:T(128)}, /*index=5*/s32[]{:T(128)}, ...), condition=%wide.region_10.11_spmd, body=%wide.region_9.10_spmd.sunk | while | flops 196867 | bytes 69741 | solution.py:77
  597.2 1.5 fusion.68
  599.3 1.5 fusion.68
  601.4 1.5 fusion.68
  603.5 1.5 fusion.68
  605.7 1.5 fusion.68
  607.8 1.5 fusion.68
  609.9 1.5 fusion.68
  612.1 1.5 fusion.68
  614.2 1.5 fusion.68
  616.3 1.5 fusion.68
  618.4 1.5 fusion.68
  620.6 1.5 fusion.68
  622.7 1.5 fusion.68
  629.1 1.5 fusion.68
  682.1 1.5 fusion.68
  684.2 1.5 fusion.68
  686.3 1.5 fusion.68
  688.4 1.5 fusion.68
  690.6 1.5 fusion.68
  692.7 1.5 fusion.68
  694.8 1.5 fusion.68
  696.9 1.5 fusion.68
  783.8 1.5 fusion.68
  785.9 1.5 fusion.68
  788.1 1.5 fusion.68
  794.5 1.5 fusion.68
  796.6 1.5 fusion.68
  798.7 1.5 fusion.68
  834.2 185.2 %while.97 = (s32[]{:T(128)}, f32[128,128]{1,0:T(8,128)S(1)}, f32[128,128]{1,0:T(8,128)S(1)}, f32[128,128]{0,1:T(8,128)S(1)}, s32[]{:T(128)}, /*index=5*/s32[]{:T(128)}, s32[]{:T(128)}, s32[]{:T(128)}) while((s32[]{:T(128)}, f32[128,128]{1,0:T(8,128)S(1)}, f32[128,128]{1,0:T(8,128)S(1)}, f32[128,128]{0,1:T(8,128)S(1)}, s32[]{:T(128)}, ...), condition=%wide.region_12.13_spmd, body=%wide.region_11.12_spmd.sunk | while | flops 196871 | bytes 69287 | solution.py:89
  1021.6 234.9 %all-reduce.4.cloned.1.call-done = f32[128,128]{1,0:T(8,128)} async-done(((f32[128,128]{1,0:T(8,128)}), f32[128,128]{1,0:T(8,128)}) %all-reduce.4.cloned.1.call-update) | async-done | bytes 65552 | tf_op jit(solution)/shard_map/psum | solution.py:109
  1256.5 271.6 %while.98 = (s32[]{:T(128)}, f32[128,128]{1,0:T(8,128)S(1)}, f32[128,128]{1,0:T(8,128)}, f32[128,128]{1,0:T(8,128)S(1)}, s32[]{:T(128)}, /*index=5*/s32[]{:T(128)}, s32[]{:T(128)}) while((s32[]{:T(128)}, f32[128,128]{1,0:T(8,128)S(1)}, f32[128,128]{1,0:T(8,128)}, f32[128,128]{1,0:T(8,128)S(1)}, s32[]{:T(128)}, /*index=5*/s32[]{:T(128)}, ...), condition=%wide.region_15.16_spmd, body=%wide.region_14.15_spmd.sunk | while | flops 196867 | bytes 69741 | solution.py:77
  1291.0 1.5 fusion.74
  1293.2 1.5 fusion.74
  1295.3 1.5 fusion.74
  1297.4 1.5 fusion.74
  1299.6 1.5 fusion.74
  1301.7 1.5 fusion.74
  1303.8 1.5 fusion.74
  1305.9 1.5 fusion.74
  1308.1 1.5 fusion.74
  1312.3 1.5 fusion.74
  1314.5 1.5 fusion.74
  1316.6 1.5 fusion.74
  1318.7 1.5 fusion.74
  1376.0 1.5 fusion.74
  1378.1 1.5 fusion.74
  1380.2 1.5 fusion.74
  1382.3 1.5 fusion.74
  1384.5 1.5 fusion.74
  1386.6 1.5 fusion.74
  1388.7 1.5 fusion.74
  1390.9 1.5 fusion.74
  1528.2 185.2 %while.99 = (s32[]{:T(128)}, f32[128,128]{1,0:T(8,128)S(1)}, f32[128,128]{1,0:T(8,128)S(1)}, f32[128,128]{0,1:T(8,128)S(1)}, s32[]{:T(128)}, /*index=5*/s32[]{:T(128)}, s32[]{:T(128)}, s32[]{:T(128)}) while((s32[]{:T(128)}, f32[128,128]{1,0:T(8,128)S(1)}, f32[128,128]{1,0:T(8,128)S(1)}, f32[128,128]{0,1:T(8,128)S(1)}, s32[]{:T(128)}, ...), condition=%wide.region_17.18_spmd, body=%wide.region_16.17_spmd.sunk | while | flops 196871 | bytes 69287 | solution.py:89
  (2166 shorter events, 928.5 us)
Async XLA Ops:
  7.2 75.0 %all-gather.2.cloned.1.call-start = ((), (), s32[]{:S(2)}) async-start(), calls=%async_computation.1 | async-start | bytes 1081344 | tf_op jit(solution)/shard_map/all_gather | solution.py:100
  8.7 116.0 %reduce-scatter.2.cloned.1.call-start = ((), (), s32[]{:S(2)}) async-start(), calls=%async_computation.2 | async-start | bytes 589824 | tf_op jit(solution)/shard_map/reduce_scatter | solution.py:102
  82.2 8.5 copy-start
  89.8 0.8 copy-start.3
  90.6 283.4 %all-reduce.6.cloned.1.call-start = ((), (), s32[]{:S(2)}) async-start(), calls=%async_computation.4 | async-start | bytes 262144 | tf_op jit(solution)/shard_map/psum | solution.py:104
  126.5 1130.0 %all-reduce.4.cloned.1.call-start = ((), (), s32[]{:S(2)}) async-start(), calls=%async_computation.3 | async-start | bytes 131072 | tf_op jit(solution)/shard_map/psum | solution.py:109
  375.8 643.6 %copy-start.1 = (f32[128,128]{0,1:T(8,128)S(1)}, f32[128,128]{0,1:T(8,128)}, u32[]{:S(2)}) copy-start(f32[128,128]{0,1:T(8,128)} %reduce-scatter.2.cloned.1.call-done) | copy-start | bytes 196612
  1019.7 694.6 %copy-start.2 = (f32[128,128]{1,0:T(8,128)}, f32[128,128]{1,0:T(8,128)S(1)}, u32[]{:S(2)}) copy-start(f32[128,128]{1,0:T(8,128)S(1)} %convolution_subtract_fusion.4) | copy-start | bytes 196612
Sparse Core Ops, SparseCore 0:
  11.0 71.0 all-gather.1
  90.8 33.9 reduce-scatter.1
  131.8 242.1 all-reduce.5
  1020.8 235.6 all-reduce.3
where the time goes:
time: 1740 us; the launch traced here: 1720 us
  matrix products  596 us (34%)
  waiting for transfers between devices  532 us (31%)
  local copies, waits for them, and re-layouts  399 us (23%)
  loops' own time  108 us (6%)
  blocking collectives  56.5 us (3%)
    dot_general x256, matrix products, forward(): jnp.dot(line, solved, precision=lax.Precision.HIGHEST)  379 us
    psum x1, waiting for transfers between devices, local(): lax.psum((gram(targets, targets), gram(targets, image)), ('row', 'col'))  247 us
    psum x1, waiting for transfers between devices, local(): conjugacy = lax.psum(gram(image, residual), ('row', 'col'))  235 us
    dot_general x256, matrix products, backward(): jnp.dot(line.T, solved, precision=lax.Precision.HIGHEST)  204 us
    dynamic_slice x256, local copies, waits for them, and re-layouts, backward(): pivot = lax.dynamic_slice_in_dim(line[:, 0], pos, 1, 0)[0]  151 us
    dynamic_slice x256, local copies, waits for them, and re-layouts, forward(): pivot = lax.dynamic_slice_in_dim(line[0], pos, 1, 0)[0]  151 us
    another operation x1, loops' own time, cholesky_factor(): return lax.fori_loop(0, size, step, (matrix, jnp.zeros_like(matrix)))[1]  93.8 us
    dynamic_slice x128, local copies, waits for them, and re-layouts, step(): pivot = jnp.sqrt(lax.dynamic_slice_in_dim(column, pos, 1, 0)[0])  75.3 us
  transfers between devices with their start and end apart: 4, of which 4 were waited for; matrix products, arithmetic and copies ran while one was open for 0% of the time, Pallas kernels for 0%

commit v1 on v0

v1 whole, which is shorter than its diff:
```python
import math

import jax
import jax.numpy as jnp
from jax import lax
from jax.experimental import pallas as pl
from jax.experimental.pallas import tpu as pltpu
from jax.sharding import PartitionSpec as P

F = 64
R = 128
B = 128
X, Y, Z, C = 4, 4, 8, 2
PLANE = X * Y
LINE = Z * C

ridge_weight = 0.5
kernel_gain = 2.0
sharpness = 3.0
exponent_scale = sharpness / F * math.log2(math.e)

f32 = jnp.float32
bf16 = jnp.bfloat16


def dot_exact(left, right):
    return jnp.dot(left, right, precision=lax.Precision.HIGHEST, preferred_element_type=f32)


def norm_rows(feat, rows):
    wide = feat.astype(f32)
    total = jnp.sum(wide * wide, axis=0, keepdims=True)
    high = total.astype(bf16).astype(f32)
    mid = (total - high).astype(bf16).astype(f32)
    low = (total - high - mid).astype(bf16).astype(f32)
    width = feat.shape[1]
    index = lax.broadcasted_iota(jnp.int32, (F, width), 0)
    first = 0 if rows else 3
    other = 3 if rows else 0
    sign = 1.0 if rows else -1.0
    extra = jnp.where(index == first, sign * high, 0.0)
    extra = jnp.where(index == first + 1, sign * mid, extra)
    extra = jnp.where(index == first + 2, sign * low, extra)
    extra = jnp.where((index >= other) & (index < other + 3), sign, extra)
    scaled = wide if rows else 2.0 * wide
    return jnp.concatenate([scaled, extra], axis=0)


def sweep_inverse(matrix):
    lanes = lax.broadcasted_iota(jnp.int32, (8, R), 1)
    subs = lax.broadcasted_iota(jnp.int32, (8, R), 0)
    tiles = tuple(matrix[8 * t : 8 * t + 8, :] for t in range(R // 8))

    def eight(_, tiles):
        tiles = list(tiles)
        for p in range(8):
            head = tiles[0]
            line = jnp.broadcast_to(head[p : p + 1, :], (8, R))
            inverse = 1.0 / jnp.broadcast_to(line[:, p : p + 1], (8, R))
            at = lanes == p
            scaled = jnp.where(at, -inverse, line * inverse)
            for t in range(R // 8):
                column = jnp.broadcast_to(tiles[t][:, p : p + 1], (8, R))
                tiles[t] = jnp.where(at, 0.0, tiles[t]) - column * scaled
            tiles[0] = jnp.where(subs == p, scaled, tiles[0])
        tiles = tiles[1:] + tiles[:1]
        return tuple(pltpu.roll(tile, R - 8, 1) for tile in tiles)

    tiles = lax.fori_loop(0, R // 8, eight, tiles)
    return jnp.concatenate(tiles, axis=0)


def kernel(
    feat_ref, targ_ref, coef_ref, resid_ref, dir_ref,
    block, row_feat, row_aug, col_aug, total, outgoing, incoming,
    sq_local, sq_in, sq_sum, sq_line, sq_full,
    gr_local, gr_in, gr_sum, gr_line, gr_full,
    block_recv, block_send, row_sems, image_sems, sq_sems, gr_sems,
):
    row, col = lax.axis_index("row"), lax.axis_index("col")
    x, z = row // Z, row % Z
    y, core = col // C, col % C
    here = x * Y + y

    def at_plane(step):
        tx, ty = (x + step // Y) % X, (y + step % Y) % Y
        return (tx * Z + z, ty * C + core), tx * Y + ty

    def at_plane_back(step):
        tx, ty = (x + X - step // Y) % X, (y + Y - step % Y) % Y
        return (tx * Z + z, ty * C + core)

    def at_line(step):
        tz, tc = (z + step // C) % Z, (core + step % C) % C
        return (x * Z + tz, y * C + tc)

    sibling = (row, y * C + 1 - core)
    above = (x * Z + (z + 1) % Z, col)
    below = (x * Z + (z + Z - 1) % Z, col)

    def send(src, dst, send_sem, recv_sem, device):
        pltpu.make_async_remote_copy(
            src_ref=src, dst_ref=dst, send_sem=send_sem, recv_sem=recv_sem,
            device_id=device, device_id_type=pl.DeviceIdType.MESH,
        ).start()

    def take(ref, sem):
        pltpu.make_async_copy(ref, ref, sem).wait()

    barrier = pltpu.get_barrier_semaphore()

    def greet(step, carry):
        pl.semaphore_signal(barrier, inc=1, device_id=at_plane(step)[0], device_id_type=pl.DeviceIdType.MESH)
        pl.semaphore_signal(barrier, inc=1, device_id=at_line(step), device_id_type=pl.DeviceIdType.MESH)
        return carry

    lax.fori_loop(1, PLANE, greet, 0)

    targ = targ_ref[...]
    targ_t = targ.T
    block[0, 0:F, :] = feat_ref[...]
    block[0, F : F + R, :] = targ_t.astype(bf16)
    pl.semaphore_wait(barrier, PLANE + LINE - 2)

    def forward(slot, step, device, to):
        send(block.at[slot], block.at[to], block_send.at[step], block_recv.at[to], device)

    forward(0, 0, above, 1)
    forward(0, 1, below, 5)
    forward(0, 2, sibling, 8)

    def send_feat(step, carry):
        send(block.at[0, pl.ds(0, F)], row_feat.at[step - 1], row_sems.at[0], row_sems.at[1], at_plane(step)[0])
        return carry

    lax.fori_loop(1, PLANE, send_feat, 0)

    def reduce_plane(local, arrive, sems):
        def one(step, carry):
            device, piece = at_plane(step)
            send(local.at[piece], arrive.at[step - 1], sems.at[0], sems.at[1], device)
            return carry

        lax.fori_loop(1, PLANE, one, 0)

    def sum_line(local, arrive, own, line, sems):
        take(arrive, sems.at[1])
        own[...] = local[here] + jnp.sum(arrive[...], axis=0)

        def one(step, carry):
            send(own, line.at[step - 1], sems.at[2], sems.at[3], at_line(step))
            return carry

        lax.fori_loop(1, LINE, one, 0)

    def spread_plane(own, line, full, sems):
        take(line, sems.at[3])
        full[here] = own[...] + jnp.sum(line[...], axis=0)

        def one(step, carry):
            send(full.at[here], full.at[here], sems.at[4], sems.at[5], at_plane(step)[0])
            return carry

        lax.fori_loop(1, PLANE, one, 0)

    def finish(arrive, sems):
        take(arrive, sems.at[5])

    def settle(arrive, line, sems):
        take(arrive, sems.at[0])
        take(line, sems.at[2])
        take(arrive, sems.at[4])

    squares = dot_exact(targ, targ_t)
    sq_local[...] = squares.reshape(PLANE, 8, R)
    reduce_plane(sq_local, sq_in, sq_sems)

    row_aug[0:B, :] = norm_rows(block[0, 0:F, :], True).T.astype(bf16)
    take(row_feat, row_sems.at[1])

    def augment(slot, carry):
        row_aug[pl.ds(pl.multiple_of(slot * B, B), B), :] = norm_rows(row_feat[slot - 1], True).T.astype(bf16)
        return carry

    lax.fori_loop(1, PLANE, augment, 0)

    def columns(pair):
        feats = jnp.concatenate([block[pair, 0:F, :], block[pair + 8, 0:F, :]], axis=1)
        col_aug[pair] = norm_rows(feats, False).astype(bf16)

    def product(rows, pair):
        minus = jnp.dot(rows, col_aug[pair], preferred_element_type=f32)
        entries = jnp.exp2(minus * exponent_scale).astype(bf16)
        panel = jnp.concatenate([block[pair, F : F + R, :], block[pair + 8, F : F + R, :]], axis=0)
        return jnp.dot(entries, panel, preferred_element_type=f32)

    def gathered(pairs, first):
        for pair in pairs:
            columns(pair)

        def one(slot, carry):
            where = pl.ds(pl.multiple_of(slot * B, B), B)
            rows = row_aug[where, :]
            value = None if first else total[where, :]
            for pair in pairs:
                term = product(rows, pair)
                value = term if value is None else value + term
            total[where, :] = value
            return carry

        lax.fori_loop(0, PLANE, one, 0)

    def arrived(slot):
        take(block.at[slot], block_recv.at[slot])

    arrived(1)
    forward(1, 3, above, 2)
    forward(1, 4, sibling, 9)
    arrived(5)
    forward(5, 5, below, 6)
    forward(5, 6, sibling, 13)
    arrived(8)
    gathered((0,), True)
    arrived(2)
    forward(2, 7, above, 3)
    forward(2, 8, sibling, 10)
    arrived(6)
    forward(6, 9, below, 7)
    forward(6, 10, sibling, 14)
    sum_line(sq_local, sq_in, sq_sum, sq_line, sq_sems)
    arrived(9)
    arrived(13)
    gathered((1, 5), False)
    arrived(3)
    forward(3, 11, above, 4)
    forward(3, 12, sibling, 11)
    arrived(7)
    forward(7, 13, sibling, 15)
    spread_plane(sq_sum, sq_line, sq_full, sq_sems)
    arrived(10)
    arrived(14)
    gathered((2, 6), False)
    arrived(4)
    forward(4, 14, sibling, 12)
    arrived(11)
    arrived(15)
    arrived(12)
    last = (3, 7, 4)
    for pair in last:
        columns(pair)

    def part(slot):
        where = pl.ds(pl.multiple_of(slot * B, B), B)
        rows = row_aug[where, :]
        value = total[where, :]
        for pair in last:
            value = value + product(rows, pair)
        return value

    def finish_rows(slot, carry):
        outgoing[slot - 1] = part(slot).astype(bf16)
        send(outgoing.at[slot - 1], incoming.at[slot - 1], image_sems.at[0], image_sems.at[1], at_plane_back(slot))
        return carry

    lax.fori_loop(1, PLANE, finish_rows, 0)
    own = part(0)
    take(incoming, image_sems.at[1])

    def add(slot, carry):
        return carry + incoming[slot].astype(f32)

    kernel_image_t = lax.fori_loop(0, PLANE - 1, add, own)
    image_t = ridge_weight * targ_t + kernel_gain * kernel_image_t
    image = image_t.T
    gr_local[:, 0:8, :] = dot_exact(targ, image_t).reshape(PLANE, 8, R)
    gr_local[:, 8:16, :] = dot_exact(image, image_t).reshape(PLANE, 8, R)
    reduce_plane(gr_local, gr_in, gr_sems)
    sum_line(gr_local, gr_in, gr_sum, gr_line, gr_sems)
    spread_plane(gr_sum, gr_line, gr_full, gr_sems)
    finish(sq_in, sq_sems)
    finish(gr_in, gr_sems)

    squares = sq_full[...].reshape(R, R)
    curvature = gr_full[:, 0:8, :].reshape(R, R)
    image_gram = gr_full[:, 8:16, :].reshape(R, R)
    curvature_t = curvature.T
    minus_inverse = sweep_inverse(0.5 * (curvature + curvature_t))
    step_size = -dot_exact(minus_inverse, squares)
    conjugacy = curvature_t - dot_exact(image_gram, step_size)
    correction = dot_exact(minus_inverse, conjugacy)
    step_t = step_size.T
    coef_ref[...] = dot_exact(step_t, targ)
    residual = targ - dot_exact(step_t, image)
    resid_ref[...] = residual
    dir_ref[...] = residual + dot_exact(correction.T, targ)

    take(row_feat, row_sems.at[0])
    take(incoming, image_sems.at[0])
    settle(sq_in, sq_line, sq_sems)
    settle(gr_in, gr_line, gr_sems)
    for step in range(15):
        take(block.at[0], block_send.at[step])


def local(features, targets):
    whole = jax.ShapeDtypeStruct((R, B), f32)
    vmem = pl.BlockSpec(memory_space=pltpu.VMEM)
    dma = pltpu.SemaphoreType.DMA
    return pl.pallas_call(
        kernel,
        out_shape=(whole, whole, whole),
        in_specs=[vmem, vmem],
        out_specs=(vmem, vmem, vmem),
        scratch_shapes=[
            pltpu.VMEM((LINE, F + R, B), bf16),
            pltpu.VMEM((PLANE - 1, F, B), bf16),
            pltpu.VMEM((PLANE * B, 2 * F), bf16),
            pltpu.VMEM((LINE // 2, 2 * F, 2 * B), bf16),
            pltpu.VMEM((PLANE * B, R), f32),
            pltpu.VMEM((PLANE - 1, B, R), bf16),
            pltpu.VMEM((PLANE - 1, B, R), bf16),
            pltpu.VMEM((PLANE, 8, R), f32),
            pltpu.VMEM((PLANE - 1, 8, R), f32),
            pltpu.VMEM((8, R), f32),
            pltpu.VMEM((LINE - 1, 8, R), f32),
            pltpu.VMEM((PLANE, 8, R), f32),
            pltpu.VMEM((PLANE, 16, R), f32),
            pltpu.VMEM((PLANE - 1, 16, R), f32),
            pltpu.VMEM((16, R), f32),
            pltpu.VMEM((LINE - 1, 16, R), f32),
            pltpu.VMEM((PLANE, 16, R), f32),
            dma((LINE,)),
            dma((15,)),
            dma((2,)),
            dma((2,)),
            dma((6,)),
            dma((6,)),
        ],
        compiler_params=pltpu.CompilerParams(
            collective_id=0, has_side_effects=True, vmem_limit_bytes=32 * 1024 * 1024
        ),
    )(features, targets)


def solution(mesh):
    spec = P(None, ("col", "row"))
    return jax.shard_map(
        local, mesh=mesh, in_specs=(spec, spec), out_specs=(spec, spec, spec), check_vma=False
    )
```

time: 1740 us -> 85.7 us (0.05); the launches traced: 1720 us -> 85.5 us
  matrix products: 596 us -> 0 us
  waiting for transfers between devices: 532 us -> 0 us
  local copies, waits for them, and re-layouts: 399 us -> 3.44 us
  loops' own time: 108 us -> 0 us
  Pallas kernels: 0 us -> 81.5 us
  blocking collectives: 56.5 us -> 0 us
    dot_general x520 -> x0, matrix products: 596 us -> none  [the longest x256 379 us: forward(): jnp.dot(line, solved, precision=lax.Precision.HIGHEST)]
    psum x2 -> x0, waiting for transfers between devices: 482 us -> none  [the longest x1 247 us: local(): lax.psum((gram(targets, targets), gram(targets, image)), ('row', 'col'))]
    dynamic_slice x642 -> x0, local copies, waits for them, and re-layouts: 377 us -> none  [the longest x256 151 us: backward(): pivot = lax.dynamic_slice_in_dim(line[:, 0], pos, 1, 0)[0]]
    another operation x6 -> x0, loops' own time: 108 us -> none  [the longest x1 93.8 us: cholesky_factor(): return lax.fori_loop(0, size, step, (matrix, jnp.zeros_like(matrix)))[1]]
    pallas_call x0 -> x1, Pallas kernels: none -> 81.5 us  [local(): pl.pallas_call(kernel, out_shape=(whole, whole, whole), in_specs=[vmem, v...]
    all_gather x2 -> x0, blocking collectives: 56.5 us -> none  [the longest x1 41.9 us: local(): lax.all_gather(features, 'row', axis=1, tiled=True)]
    reduce_scatter x1 -> x0, waiting for transfers between devices: 33 us -> none  [local(): lax.psum_scatter(partial_image, 'col', scatter_dimension=1, tiled=True)]
    dynamic_update_slice x640 -> x0, local copies, waits for them, and re-layouts: 20.4 us -> none  [the longest x256 7.81 us: backward(): return lax.dynamic_update_slice_in_dim(solved, value, pos, 0)]
  transfers between devices with their start and end apart: 4 -> 0, of which waited for: 4 -> 0; matrix products, arithmetic and copies ran while one was open for 0% -> 0% of each run, Pallas kernels for 0% -> 0%
where the time goes in v1:
time: 85.7 us; the launch traced here: 85.5 us
  Pallas kernels  81.5 us (95%)
  local copies, waits for them, and re-layouts  3.44 us (4%)
    pallas_call x1, Pallas kernels, local(): pl.pallas_call(kernel, out_shape=(whole, whole, whole), in_specs=[vmem, v...  81.5 us
    unnamed x7, local copies, waits for them, and re-layouts  3.44 us

profile of v1, /device:TPU:1, one launch (start us, length us, event | category | flops | bytes accessed | tf_op | source)
XLA Modules:
  0.0 85.5 jit_solution(11191255972636845273)
XLA Ops:
  0.6 0.0 copy-start
  0.6 0.8 copy-done
  1.5 0.0 copy-start.1
  1.5 0.7 copy-done.1
  2.2 81.5 %shard_map.49 = (f32[128,128]{1,0:T(8,128)S(1)}, f32[128,128]{1,0:T(8,128)S(1)}, f32[128,128]{1,0:T(8,128)S(1)}) custom-call(bf16[64,128]{1,0:T(8,128)(2,1)S(1)} %copy-done.1, f32[128,128]{1,0:T(8,128)S(1)} %copy-done), custom_call_target="tpu_custom_call" | custom-call | tf_op jit(solution)/shard_map/pallas_call | solution.py:309
  83.7 0.6 copy.8
  84.3 0.6 copy.9
  84.9 0.6 copy.10
Async XLA Ops:
  0.6 0.8 copy-start
  1.5 0.7 copy-start.1

commit v2 on v1

--- a/solution.py
+++ b/solution.py
@@ -13,6 +13,7 @@
 X, Y, Z, C = 4, 4, 8, 2
 PLANE = X * Y
 LINE = Z * C
+EARLY = 5
 
 ridge_weight = 0.5
 kernel_gain = 2.0
@@ -49,25 +50,48 @@
 def sweep_inverse(matrix):
     lanes = lax.broadcasted_iota(jnp.int32, (8, R), 1)
     subs = lax.broadcasted_iota(jnp.int32, (8, R), 0)
+    low = lanes < 8
+
+    def spread_lane(tile, lane):
+        return jnp.broadcast_to(tile[:, lane : lane + 1], (8, R))
+
+    def spread_line(tile, sub):
+        return jnp.broadcast_to(tile[sub : sub + 1, :], (8, R))
+
+    def eight(_, tiles):
+        head = tiles[0]
+        cols = [spread_lane(head, p) for p in range(8)]
+        pivot = {(s, t): spread_line(cols[t], s) for t in range(8) for s in range(t + 1)}
+        rows = [jnp.where(low, jnp.where(lanes == p, -1.0, 0.0), spread_line(head, p)) for p in range(8)]
+        for p in range(8):
+            inverse = 1.0 / pivot[p, p]
+            rows[p] = rows[p] * inverse
+            ahead = {t: pivot[p, t] * inverse for t in range(p + 1, 8)}
+            for s in range(8):
+                if s != p:
+                    rows[s] = rows[s] - pivot[min(s, p), max(s, p)] * rows[p]
+            for t in range(p + 1, 8):
+                for s in range(t + 1):
+                    if s < p:
+                        pivot[s, t] = pivot[s, t] - pivot[s, p] * ahead[t]
+                    elif s > p:
+                        pivot[s, t] = pivot[s, t] - pivot[p, s] * ahead[t]
+            for t in ahead:
+                pivot[p, t] = ahead[t]
+        turned = []
+        for tile in tiles[1:]:
+            terms = [spread_lane(tile, p) * rows[p] for p in range(8)]
+            while len(terms) > 1:
+                terms = [terms[k] + terms[k + 1] for k in range(0, len(terms), 2)]
+            turned.append(jnp.where(low, 0.0, tile) - terms[0])
+        swept = rows[7]
+        for p in range(7):
+            swept = jnp.where(subs == p, rows[p], swept)
+        turned.append(swept)
+        return tuple(pltpu.roll(tile, R - 8, 1) for tile in turned)
+
     tiles = tuple(matrix[8 * t : 8 * t + 8, :] for t in range(R // 8))
-
-    def eight(_, tiles):
-        tiles = list(tiles)
-        for p in range(8):
-            head = tiles[0]
-            line = jnp.broadcast_to(head[p : p + 1, :], (8, R))
-            inverse = 1.0 / jnp.broadcast_to(line[:, p : p + 1], (8, R))
-            at = lanes == p
-            scaled = jnp.where(at, -inverse, line * inverse)
-            for t in range(R // 8):
-                column = jnp.broadcast_to(tiles[t][:, p : p + 1], (8, R))
-                tiles[t] = jnp.where(at, 0.0, tiles[t]) - column * scaled
-            tiles[0] = jnp.where(subs == p, scaled, tiles[0])
-        tiles = tiles[1:] + tiles[:1]
-        return tuple(pltpu.roll(tile, R - 8, 1) for tile in tiles)
-
-    tiles = lax.fori_loop(0, R // 8, eight, tiles)
-    return jnp.concatenate(tiles, axis=0)
+    return jnp.concatenate(lax.fori_loop(0, R // 8, eight, tiles), axis=0)
 
 
 def kernel(
@@ -75,7 +99,7 @@
     block, row_feat, row_aug, col_aug, total, outgoing, incoming,
     sq_local, sq_in, sq_sum, sq_line, sq_full,
     gr_local, gr_in, gr_sum, gr_line, gr_full,
-    block_recv, block_send, row_sems, image_sems, sq_sems, gr_sems,
+    block_recv, cross_send, line_send, row_sems, image_sems, sq_sems, gr_sems,
 ):
     row, col = lax.axis_index("row"), lax.axis_index("col")
     x, z = row // Z, row % Z
@@ -95,8 +119,9 @@
         return (x * Z + tz, y * C + tc)
 
     sibling = (row, y * C + 1 - core)
-    above = (x * Z + (z + 1) % Z, col)
-    below = (x * Z + (z + Z - 1) % Z, col)
+
+    def up(step):
+        return (x * Z + (z + step) % Z, col)
 
     def send(src, dst, send_sem, recv_sem, device):
         pltpu.make_async_remote_copy(
@@ -120,20 +145,29 @@
     targ_t = targ.T
     block[0, 0:F, :] = feat_ref[...]
     block[0, F : F + R, :] = targ_t.astype(bf16)
+    squares = dot_exact(targ, targ_t)
+    sq_local[...] = squares.reshape(PLANE, 8, R)
+    row_aug[0:B, :] = norm_rows(block[0, 0:F, :], True).T.astype(bf16)
     pl.semaphore_wait(barrier, PLANE + LINE - 2)
 
-    def forward(slot, step, device, to):
-        send(block.at[slot], block.at[to], block_send.at[step], block_recv.at[to], device)
-
-    forward(0, 0, above, 1)
-    forward(0, 1, below, 5)
-    forward(0, 2, sibling, 8)
+    def order(step):
+        return jnp.where(step % 2 == 1, (step + 1) // 2, (Z - step // 2) % Z)
+
+    def across(slot):
+        send(block.at[slot], block.at[slot + Z], cross_send.at[slot], block_recv.at[slot + Z], sibling)
+
+    def send_block(step, carry):
+        slot = order(step)
+        send(block.at[0], block.at[slot], line_send.at[0], block_recv.at[slot], up(slot))
+        return carry
 
     def send_feat(step, carry):
         send(block.at[0, pl.ds(0, F)], row_feat.at[step - 1], row_sems.at[0], row_sems.at[1], at_plane(step)[0])
         return carry
 
+    across(0)
     lax.fori_loop(1, PLANE, send_feat, 0)
+    lax.fori_loop(1, Z, send_block, 0)
 
     def reduce_plane(local, arrive, sems):
         def one(step, carry):
@@ -171,11 +205,17 @@
         take(line, sems.at[2])
         take(arrive, sems.at[4])
 
-    squares = dot_exact(targ, targ_t)
-    sq_local[...] = squares.reshape(PLANE, 8, R)
     reduce_plane(sq_local, sq_in, sq_sems)
 
-    row_aug[0:B, :] = norm_rows(block[0, 0:F, :], True).T.astype(bf16)
+    def arrived(slot):
+        take(block.at[slot], block_recv.at[slot])
+
+    def pass_on(step, carry):
+        arrived(order(step))
+        across(order(step))
+        return carry
+
+    lax.fori_loop(1, 3, pass_on, 0)
     take(row_feat, row_sems.at[1])
 
     def augment(slot, carry):
@@ -185,91 +225,65 @@
     lax.fori_loop(1, PLANE, augment, 0)
 
     def columns(pair):
-        feats = jnp.concatenate([block[pair, 0:F, :], block[pair + 8, 0:F, :]], axis=1)
+        arrived(pair + Z)
+        feats = jnp.concatenate([block[pair, 0:F, :], block[pair + Z, 0:F, :]], axis=1)
         col_aug[pair] = norm_rows(feats, False).astype(bf16)
 
     def product(rows, pair):
         minus = jnp.dot(rows, col_aug[pair], preferred_element_type=f32)
         entries = jnp.exp2(minus * exponent_scale).astype(bf16)
-        panel = jnp.concatenate([block[pair, F : F + R, :], block[pair + 8, F : F + R, :]], axis=0)
+        panel = jnp.concatenate([block[pair, F : F + R, :], block[pair + Z, F : F + R, :]], axis=0)
         return jnp.dot(entries, panel, preferred_element_type=f32)
 
-    def gathered(pairs, first):
-        for pair in pairs:
-            columns(pair)
-
-        def one(slot, carry):
-            where = pl.ds(pl.multiple_of(slot * B, B), B)
-            rows = row_aug[where, :]
-            value = None if first else total[where, :]
-            for pair in pairs:
-                term = product(rows, pair)
-                value = term if value is None else value + term
-            total[where, :] = value
-            return carry
-
-        lax.fori_loop(0, PLANE, one, 0)
-
-    def arrived(slot):
-        take(block.at[slot], block_recv.at[slot])
-
-    arrived(1)
-    forward(1, 3, above, 2)
-    forward(1, 4, sibling, 9)
-    arrived(5)
-    forward(5, 5, below, 6)
-    forward(5, 6, sibling, 13)
-    arrived(8)
-    gathered((0,), True)
-    arrived(2)
-    forward(2, 7, above, 3)
-    forward(2, 8, sibling, 10)
-    arrived(6)
-    forward(6, 9, below, 7)
-    forward(6, 10, sibling, 14)
+    def gathered(step, carry):
+        pair = order(step)
+        columns(pair)
+        total[...] += product(row_aug[...], pair)
+        return carry
+
+    columns(0)
+    total[...] = product(row_aug[...], 0)
+    lax.fori_loop(3, EARLY, pass_on, 0)
+    lax.fori_loop(1, 3, gathered, 0)
+    lax.fori_loop(EARLY, Z, pass_on, 0)
+    lax.fori_loop(3, EARLY, gathered, 0)
     sum_line(sq_local, sq_in, sq_sum, sq_line, sq_sems)
-    arrived(9)
-    arrived(13)
-    gathered((1, 5), False)
-    arrived(3)
-    forward(3, 11, above, 4)
-    forward(3, 12, sibling, 11)
-    arrived(7)
-    forward(7, 13, sibling, 15)
-    spread_plane(sq_sum, sq_line, sq_full, sq_sems)
-    arrived(10)
-    arrived(14)
-    gathered((2, 6), False)
-    arrived(4)
-    forward(4, 14, sibling, 12)
-    arrived(11)
-    arrived(15)
-    arrived(12)
-    last = (3, 7, 4)
+    last = [(step + 1) // 2 if step % 2 else Z - step // 2 for step in range(EARLY, Z)]
     for pair in last:
         columns(pair)
 
-    def part(slot):
-        where = pl.ds(pl.multiple_of(slot * B, B), B)
+    def part(dx):
+        where = pl.ds(pl.multiple_of(dx * Y * B, Y * B), Y * B)
         rows = row_aug[where, :]
         value = total[where, :]
         for pair in last:
             value = value + product(rows, pair)
         return value
 
-    def finish_rows(slot, carry):
-        outgoing[slot - 1] = part(slot).astype(bf16)
-        send(outgoing.at[slot - 1], incoming.at[slot - 1], image_sems.at[0], image_sems.at[1], at_plane_back(slot))
-        return carry
-
-    lax.fori_loop(1, PLANE, finish_rows, 0)
+    def send_rows(slot):
+        send(outgoing.at[slot], incoming.at[slot], image_sems.at[0], image_sems.at[1], at_plane_back(slot))
+
+    def finish_rows(step, carry):
+        dx = 2 + step - 3 * (step // 2)
+        outgoing[pl.ds(dx * Y, Y)] = part(dx).astype(bf16).reshape(Y, B, R)
+        for dy in (2, 1, 3, 0):
+            send_rows(dx * Y + dy)
+        return carry
+
+    lax.fori_loop(0, X - 1, finish_rows, 0)
     own = part(0)
-    take(incoming, image_sems.at[1])
+    outgoing[pl.ds(0, Y)] = own.astype(bf16).reshape(Y, B, R)
+    for dy in (2, 1, 3):
+        send_rows(dy)
+    own = own[0:B, :]
+    spread_plane(sq_sum, sq_line, sq_full, sq_sems)
+    others = incoming.at[pl.ds(1, PLANE - 1)]
+    take(others, image_sems.at[1])
 
     def add(slot, carry):
         return carry + incoming[slot].astype(f32)
 
-    kernel_image_t = lax.fori_loop(0, PLANE - 1, add, own)
+    kernel_image_t = lax.fori_loop(1, PLANE, add, own)
     image_t = ridge_weight * targ_t + kernel_gain * kernel_image_t
     image = image_t.T
     gr_local[:, 0:8, :] = dot_exact(targ, image_t).reshape(PLANE, 8, R)
@@ -295,11 +309,12 @@
     dir_ref[...] = residual + dot_exact(correction.T, targ)
 
     take(row_feat, row_sems.at[0])
-    take(incoming, image_sems.at[0])
+    take(others, image_sems.at[0])
     settle(sq_in, sq_line, sq_sems)
     settle(gr_in, gr_line, gr_sems)
-    for step in range(15):
-        take(block.at[0], block_send.at[step])
+    take(block.at[pl.ds(1, Z - 1)], line_send.at[0])
+    for slot in range(Z):
+        take(block.at[slot], cross_send.at[slot])
 
 
 def local(features, targets):
@@ -317,8 +332,8 @@
             pltpu.VMEM((PLANE * B, 2 * F), bf16),
             pltpu.VMEM((LINE // 2, 2 * F, 2 * B), bf16),
             pltpu.VMEM((PLANE * B, R), f32),
-            pltpu.VMEM((PLANE - 1, B, R), bf16),
-            pltpu.VMEM((PLANE - 1, B, R), bf16),
+            pltpu.VMEM((PLANE, B, R), bf16),
+            pltpu.VMEM((PLANE, B, R), bf16),
             pltpu.VMEM((PLANE, 8, R), f32),
             pltpu.VMEM((PLANE - 1, 8, R), f32),
             pltpu.VMEM((8, R), f32),
@@ -330,7 +345,8 @@
             pltpu.VMEM((LINE - 1, 16, R), f32),
             pltpu.VMEM((PLANE, 16, R), f32),
             dma((LINE,)),
-            dma((15,)),
+            dma((Z,)),
+            dma((1,)),
             dma((2,)),
             dma((2,)),
             dma((6,)),

time: 85.7 us -> 62.4 us (0.73)
  Pallas kernels: 81.5 us -> 58.2 us
    pallas_call x1, Pallas kernels: 81.5 us -> 58.2 us  [local(): pl.pallas_call(kernel, out_shape=(whole, whole, whole), in_specs=[vmem, v...]
where the time goes in v2:
time: 62.4 us; the launch traced here: 62.2 us
  Pallas kernels  58.2 us (93%)
  local copies, waits for them, and re-layouts  3.44 us (6%)
  between operations  0.65 us (1%)
    pallas_call x1, Pallas kernels, local(): pl.pallas_call(kernel, out_shape=(whole, whole, whole), in_specs=[vmem, v...  58.2 us
    unnamed x7, local copies, waits for them, and re-layouts  3.44 us

profile of v2, /device:TPU:1, one launch (start us, length us, event | category | flops | bytes accessed | tf_op | source)
XLA Modules:
  0.0 62.2 jit_solution(13815454613047174075)
XLA Ops:
  0.6 0.0 copy-start
  0.6 0.8 %copy-done = f32[128,128]{1,0:T(8,128)S(1)} copy-done((f32[128,128]{1,0:T(8,128)S(1)}, f32[128,128]{1,0:T(8,128)}, u32[]{:S(2)}) %copy-start) | copy-done | bytes 65560
  1.5 0.0 copy-start.1
  1.5 0.7 %copy-done.1 = bf16[64,128]{1,0:T(8,128)(2,1)S(1)} copy-done((bf16[64,128]{1,0:T(8,128)(2,1)S(1)}, bf16[64,128]{1,0:T(8,128)(2,1)}, u32[]{:S(2)}) %copy-start.1) | copy-done | bytes 16408
  2.2 58.2 %shard_map.49 = (f32[128,128]{1,0:T(8,128)S(1)}, f32[128,128]{1,0:T(8,128)S(1)}, f32[128,128]{1,0:T(8,128)S(1)}) custom-call(bf16[64,128]{1,0:T(8,128)(2,1)S(1)} %copy-done.1, f32[128,128]{1,0:T(8,128)S(1)} %copy-done), custom_call_target="tpu_custom_call" | custom-call | tf_op jit(solution)/shard_map/pallas_call | solution.py:324
  60.4 0.6 %copy.8 = f32[128,128]{1,0:T(8,128)} copy(f32[128,128]{1,0:T(8,128)S(1)} %get-tuple-element.6) | data formatting | bytes 131072
  61.0 0.6 %copy.9 = f32[128,128]{1,0:T(8,128)} copy(f32[128,128]{1,0:T(8,128)S(1)} %get-tuple-element.7) | data formatting | bytes 131072
  61.6 0.6 %copy.10 = f32[128,128]{1,0:T(8,128)} copy(f32[128,128]{1,0:T(8,128)S(1)} %get-tuple-element.8) | data formatting | bytes 131072
Async XLA Ops:
  0.6 0.8 %copy-start = (f32[128,128]{1,0:T(8,128)S(1)}, f32[128,128]{1,0:T(8,128)}, u32[]{:S(2)}) copy-start(f32[128,128]{1,0:T(8,128)} %targ_ref.1) | copy-start | bytes 196612
  1.5 0.7 %copy-start.1 = (bf16[64,128]{1,0:T(8,128)(2,1)S(1)}, bf16[64,128]{1,0:T(8,128)(2,1)}, u32[]{:S(2)}) copy-start(bf16[64,128]{1,0:T(8,128)(2,1)} %feat_ref.1) | copy-start | bytes 49156

commit v3 on v2

--- a/solution.py
+++ b/solution.py
@@ -14,6 +14,7 @@
 PLANE = X * Y
 LINE = Z * C
 EARLY = 5
+VMEMLIM = 60
 
 ridge_weight = 0.5
 kernel_gain = 2.0
@@ -91,15 +92,16 @@
         return tuple(pltpu.roll(tile, R - 8, 1) for tile in turned)
 
     tiles = tuple(matrix[8 * t : 8 * t + 8, :] for t in range(R // 8))
-    return jnp.concatenate(lax.fori_loop(0, R // 8, eight, tiles), axis=0)
+    return jnp.concatenate(lax.fori_loop(0, R // 8, eight, tiles, unroll=4), axis=0)
 
 
 def kernel(
-    feat_ref, targ_ref, coef_ref, resid_ref, dir_ref,
-    block, row_feat, row_aug, col_aug, total, outgoing, incoming,
+    feat_ref, targ_ref, coef_ref, taken_ref, added_ref,
+    targ_own, block, row_feat, row_targ, row_aug, col_aug, total, outgoing, incoming,
     sq_local, sq_in, sq_sum, sq_line, sq_full,
+    cu_local, cu_in, cu_sum, cu_line, cu_full,
     gr_local, gr_in, gr_sum, gr_line, gr_full,
-    block_recv, cross_send, line_send, row_sems, image_sems, sq_sems, gr_sems,
+    load_sems, block_recv, cross_send, line_send, row_recv, row_send, targ_sems, image_sems, sq_sems, cu_sems, gr_sems,
 ):
     row, col = lax.axis_index("row"), lax.axis_index("col")
     x, z = row // Z, row % Z
@@ -141,13 +143,17 @@
 
     lax.fori_loop(1, PLANE, greet, 0)
 
-    targ = targ_ref[...]
+    load_feat = pltpu.make_async_copy(feat_ref, block.at[0, pl.ds(0, F)], load_sems.at[0])
+    load_targ = pltpu.make_async_copy(targ_ref, targ_own, load_sems.at[1])
+    load_targ.start()
+    load_feat.start()
+    load_targ.wait()
+    load_feat.wait()
+    targ = targ_own[...]
     targ_t = targ.T
-    block[0, 0:F, :] = feat_ref[...]
+    targ_high = targ.astype(bf16)
+    row_targ[0] = targ_high
     block[0, F : F + R, :] = targ_t.astype(bf16)
-    squares = dot_exact(targ, targ_t)
-    sq_local[...] = squares.reshape(PLANE, 8, R)
-    row_aug[0:B, :] = norm_rows(block[0, 0:F, :], True).T.astype(bf16)
     pl.semaphore_wait(barrier, PLANE + LINE - 2)
 
     def order(step):
@@ -156,18 +162,26 @@
     def across(slot):
         send(block.at[slot], block.at[slot + Z], cross_send.at[slot], block_recv.at[slot + Z], sibling)
 
-    def send_block(step, carry):
-        slot = order(step)
+    def send_block(slot):
         send(block.at[0], block.at[slot], line_send.at[0], block_recv.at[slot], up(slot))
-        return carry
+
+    def plane_order(step):
+        turn = step // Y
+        return (turn + turn // 2 - 2 * (turn // 3)) * Y + step % Y
 
     def send_feat(step, carry):
-        send(block.at[0, pl.ds(0, F)], row_feat.at[step - 1], row_sems.at[0], row_sems.at[1], at_plane(step)[0])
-        return carry
-
+        slot = plane_order(PLANE - step)
+        send(block.at[0, pl.ds(0, F)], row_feat.at[slot], row_send.at[0], row_recv.at[slot], at_plane(slot)[0])
+        return carry
+
+    def send_targ(step, carry):
+        send(row_targ.at[0], row_targ.at[step], targ_sems.at[0], targ_sems.at[1], at_plane(step)[0])
+        return carry
+
+    for slot in (2, Z - 2, 1, Z - 1):
+        send_block(slot)
+    lax.fori_loop(1, PLANE, send_feat, 0)
     across(0)
-    lax.fori_loop(1, PLANE, send_feat, 0)
-    lax.fori_loop(1, Z, send_block, 0)
 
     def reduce_plane(local, arrive, sems):
         def one(step, carry):
@@ -205,7 +219,10 @@
         take(line, sems.at[2])
         take(arrive, sems.at[4])
 
+    sq_local[...] = dot_exact(targ, targ_t).reshape(PLANE, 8, R)
     reduce_plane(sq_local, sq_in, sq_sems)
+    lax.fori_loop(1, PLANE, send_targ, 0)
+    row_aug[0:B, :] = norm_rows(block[0, 0:F, :], True).T.astype(bf16)
 
     def arrived(slot):
         take(block.at[slot], block_recv.at[slot])
@@ -215,14 +232,24 @@
         across(order(step))
         return carry
 
-    lax.fori_loop(1, 3, pass_on, 0)
-    take(row_feat, row_sems.at[1])
-
-    def augment(slot, carry):
-        row_aug[pl.ds(pl.multiple_of(slot * B, B), B), :] = norm_rows(row_feat[slot - 1], True).T.astype(bf16)
-        return carry
-
-    lax.fori_loop(1, PLANE, augment, 0)
+
+    def augment(step, carry):
+        slot = plane_order(step)
+        take(row_feat.at[slot], row_recv.at[slot])
+        row_aug[pl.ds(pl.multiple_of(slot * B, B), B), :] = norm_rows(row_feat[slot], True).T.astype(bf16)
+        return carry
+
+    lax.fori_loop(1, PLANE // 2, augment, 0)
+
+    half = (F + R) // 2
+    for slot, direction, first in ((2, 1, 0), (Z - 2, Z - 1, half)):
+        arrived(slot)
+        to = (slot + direction) % Z
+        send(block.at[slot], block.at[to], line_send.at[1], block_recv.at[to], up(direction))
+        rows = pl.ds(first, half)
+        send(block.at[slot, rows], block.at[4, rows], line_send.at[1], block_recv.at[4], up(slot))
+        across(slot)
+    lax.fori_loop(PLANE // 2, PLANE, augment, 0)
 
     def columns(pair):
         arrived(pair + Z)
@@ -241,12 +268,12 @@
         total[...] += product(row_aug[...], pair)
         return carry
 
+    lax.fori_loop(1, 3, pass_on, 0)
     columns(0)
     total[...] = product(row_aug[...], 0)
-    lax.fori_loop(3, EARLY, pass_on, 0)
-    lax.fori_loop(1, 3, gathered, 0)
+    lax.fori_loop(1, EARLY - 1, gathered, 0)
     lax.fori_loop(EARLY, Z, pass_on, 0)
-    lax.fori_loop(3, EARLY, gathered, 0)
+    lax.fori_loop(EARLY - 1, EARLY, gathered, 0)
     sum_line(sq_local, sq_in, sq_sum, sq_line, sq_sems)
     last = [(step + 1) // 2 if step % 2 else Z - step // 2 for step in range(EARLY, Z)]
     for pair in last:
@@ -272,11 +299,18 @@
 
     lax.fori_loop(0, X - 1, finish_rows, 0)
     own = part(0)
-    outgoing[pl.ds(0, Y)] = own.astype(bf16).reshape(Y, B, R)
+    outgoing[pl.ds(1, Y - 1)] = own[B:, :].astype(bf16).reshape(Y - 1, B, R)
     for dy in (2, 1, 3):
         send_rows(dy)
     own = own[0:B, :]
-    spread_plane(sq_sum, sq_line, sq_full, sq_sems)
+    row_targs = row_targ.at[pl.ds(1, PLANE - 1)]
+    take(row_targs, targ_sems.at[1])
+    targs = jnp.concatenate([row_targ[slot] for slot in range(1, PLANE)], axis=1)
+    images = outgoing[pl.ds(1, PLANE - 1)].reshape((PLANE - 1) * B, R)
+    term = dot_exact(targ, own) + jnp.dot(targs, images, preferred_element_type=f32)
+    cu_local[...] = ridge_weight * sq_local[...] + kernel_gain * term.reshape(PLANE, 8, R)
+    reduce_plane(cu_local, cu_in, cu_sems)
+
     others = incoming.at[pl.ds(1, PLANE - 1)]
     take(others, image_sems.at[1])
 
@@ -286,33 +320,38 @@
     kernel_image_t = lax.fori_loop(1, PLANE, add, own)
     image_t = ridge_weight * targ_t + kernel_gain * kernel_image_t
     image = image_t.T
-    gr_local[:, 0:8, :] = dot_exact(targ, image_t).reshape(PLANE, 8, R)
-    gr_local[:, 8:16, :] = dot_exact(image, image_t).reshape(PLANE, 8, R)
+    gr_local[...] = dot_exact(image, image_t).reshape(PLANE, 8, R)
     reduce_plane(gr_local, gr_in, gr_sems)
+    sum_line(cu_local, cu_in, cu_sum, cu_line, cu_sems)
+    spread_plane(sq_sum, sq_line, sq_full, sq_sems)
     sum_line(gr_local, gr_in, gr_sum, gr_line, gr_sems)
+    spread_plane(cu_sum, cu_line, cu_full, cu_sems)
     spread_plane(gr_sum, gr_line, gr_full, gr_sems)
-    finish(sq_in, sq_sems)
-    finish(gr_in, gr_sems)
-
-    squares = sq_full[...].reshape(R, R)
-    curvature = gr_full[:, 0:8, :].reshape(R, R)
-    image_gram = gr_full[:, 8:16, :].reshape(R, R)
+
+    finish(cu_in, cu_sems)
+    curvature = cu_full[...].reshape(R, R)
     curvature_t = curvature.T
     minus_inverse = sweep_inverse(0.5 * (curvature + curvature_t))
+    finish(sq_in, sq_sems)
+    squares = sq_full[...].reshape(R, R)
     step_size = -dot_exact(minus_inverse, squares)
-    conjugacy = curvature_t - dot_exact(image_gram, step_size)
-    correction = dot_exact(minus_inverse, conjugacy)
     step_t = step_size.T
     coef_ref[...] = dot_exact(step_t, targ)
-    residual = targ - dot_exact(step_t, image)
-    resid_ref[...] = residual
-    dir_ref[...] = residual + dot_exact(correction.T, targ)
-
-    take(row_feat, row_sems.at[0])
+    taken_ref[...] = dot_exact(step_t, image)
+    solved = dot_exact(minus_inverse, targ)
+    before = dot_exact(curvature, solved)
+    finish(gr_in, gr_sems)
+    image_gram = gr_full[...].reshape(R, R)
+    added_ref[...] = before - dot_exact(step_t, dot_exact(image_gram, solved))
+
+    take(row_feat.at[pl.ds(1, PLANE - 1)], row_send.at[0])
+    take(row_targs, targ_sems.at[0])
     take(others, image_sems.at[0])
     settle(sq_in, sq_line, sq_sems)
+    settle(cu_in, cu_line, cu_sems)
     settle(gr_in, gr_line, gr_sems)
-    take(block.at[pl.ds(1, Z - 1)], line_send.at[0])
+    take(block.at[pl.ds(1, 4)], line_send.at[0])
+    take(block.at[pl.ds(1, 3)], line_send.at[1])
     for slot in range(Z):
         take(block.at[slot], cross_send.at[slot])
 
@@ -320,42 +359,49 @@
 def local(features, targets):
     whole = jax.ShapeDtypeStruct((R, B), f32)
     vmem = pl.BlockSpec(memory_space=pltpu.VMEM)
+    hbm = pl.BlockSpec(memory_space=pltpu.HBM)
     dma = pltpu.SemaphoreType.DMA
-    return pl.pallas_call(
+    sums = [
+        pltpu.VMEM((PLANE, 8, R), f32),
+        pltpu.VMEM((PLANE - 1, 8, R), f32),
+        pltpu.VMEM((8, R), f32),
+        pltpu.VMEM((LINE - 1, 8, R), f32),
+        pltpu.VMEM((PLANE, 8, R), f32),
+    ]
+    coefficients, taken, added = pl.pallas_call(
         kernel,
         out_shape=(whole, whole, whole),
-        in_specs=[vmem, vmem],
+        in_specs=[hbm, hbm],
         out_specs=(vmem, vmem, vmem),
         scratch_shapes=[
+            pltpu.VMEM((R, B), f32),
             pltpu.VMEM((LINE, F + R, B), bf16),
-            pltpu.VMEM((PLANE - 1, F, B), bf16),
+            pltpu.VMEM((PLANE, F, B), bf16),
+            pltpu.VMEM((PLANE, R, B), bf16),
             pltpu.VMEM((PLANE * B, 2 * F), bf16),
             pltpu.VMEM((LINE // 2, 2 * F, 2 * B), bf16),
             pltpu.VMEM((PLANE * B, R), f32),
             pltpu.VMEM((PLANE, B, R), bf16),
             pltpu.VMEM((PLANE, B, R), bf16),
-            pltpu.VMEM((PLANE, 8, R), f32),
-            pltpu.VMEM((PLANE - 1, 8, R), f32),
-            pltpu.VMEM((8, R), f32),
-            pltpu.VMEM((LINE - 1, 8, R), f32),
-            pltpu.VMEM((PLANE, 8, R), f32),
-            pltpu.VMEM((PLANE, 16, R), f32),
-            pltpu.VMEM((PLANE - 1, 16, R), f32),
-            pltpu.VMEM((16, R), f32),
-            pltpu.VMEM((LINE - 1, 16, R), f32),
-            pltpu.VMEM((PLANE, 16, R), f32),
+            *sums, *sums, *sums,
+            dma((2,)),
             dma((LINE,)),
             dma((Z,)),
+            dma((2,)),
+            dma((PLANE,)),
             dma((1,)),
             dma((2,)),
             dma((2,)),
             dma((6,)),
             dma((6,)),
+            dma((6,)),
         ],
         compiler_params=pltpu.CompilerParams(
-            collective_id=0, has_side_effects=True, vmem_limit_bytes=32 * 1024 * 1024
+            collective_id=0, has_side_effects=True, vmem_limit_bytes=VMEMLIM * 1024 * 1024
         ),
     )(features, targets)
+    residual = targets - taken
+    return coefficients, residual, residual + added
 
 
 def solution(mesh):

time: 62.4 us -> 57 us (0.913)
  Pallas kernels: 58.2 us -> 54 us
  local copies, waits for them, and re-layouts: 3.44 us -> 0.64 us
  other arithmetic: 0 us -> 1.56 us
    pallas_call x1, Pallas kernels: 58.2 us -> 54 us  [local(): pl.pallas_call(kernel, out_shape=(whole, whole, whole), in_specs=[hbm, hb...]
    unnamed x7 -> x5, local copies, waits for them, and re-layouts: 3.44 us -> 0.64 us
    add x0 -> x1, other arithmetic: none -> 1.56 us  [local(): return (coefficients, residual, residual + added)]
where the time goes in v3:
time: 57 us; the launch traced here: 56.8 us
  Pallas kernels  54 us (95%)
  other arithmetic  1.56 us (3%)
  between operations  0.66 us (1%)
  local copies, waits for them, and re-layouts  0.64 us (1%)
    pallas_call x1, Pallas kernels, local(): pl.pallas_call(kernel, out_shape=(whole, whole, whole), in_specs=[hbm, hb...  54 us
    add x1, other arithmetic, local(): return (coefficients, residual, residual + added)  1.56 us

profile of v3, /device:TPU:1, one launch (start us, length us, event | category | flops | bytes accessed | tf_op | source)
XLA Modules:
  0.0 56.8 jit_solution(10530090721355052070)
XLA Ops:
  0.6 0.0 copy-start
  0.6 54.0 %shard_map.49 = (f32[128,128]{1,0:T(8,128)}, f32[128,128]{1,0:T(8,128)}, f32[128,128]{1,0:T(8,128)}) custom-call(bf16[64,128]{1,0:T(8,128)(2,1)} %feat_ref.1, f32[128,128]{1,0:T(8,128)} %targ_ref.1), custom_call_target="tpu_custom_call" | custom-call | tf_op jit(solution)/shard_map/pallas_call | solution.py:371
  54.6 0.0 copy-done
  54.6 0.0 copy-start.1
  54.6 1.6 %fusion = (f32[128,128]{1,0:T(8,128)}, f32[128,128]{1,0:T(8,128)}) fusion(f32[128,128]{1,0:T(8,128)} %get-tuple-element.8, f32[128,128]{1,0:T(8,128)S(1)} %copy-done, f32[128,128]{1,0:T(8,128)} %get-tuple-element.7), kind=kLoop, calls=%fused_computation | loop fusion | flops 32768 | bytes 327680 | tf_op jit(solution)/shard_map/add | solution.py:404
  56.2 0.0 copy-done.1
  56.2 0.6 %copy.6 = f32[128,128]{1,0:T(8,128)} copy(f32[128,128]{1,0:T(8,128)S(1)} %copy-done.1) | data formatting | bytes 131072
Async XLA Ops:
  0.6 54.0 %copy-start = (f32[128,128]{1,0:T(8,128)S(1)}, f32[128,128]{1,0:T(8,128)}, u32[]{:S(2)}) copy-start(f32[128,128]{1,0:T(8,128)} %targ_ref.1) | copy-start | bytes 196612
  54.6 1.6 %copy-start.1 = (f32[128,128]{1,0:T(8,128)S(1)}, f32[128,128]{1,0:T(8,128)}, u32[]{:S(2)}) copy-start(f32[128,128]{1,0:T(8,128)} %get-tuple-element.14) | copy-start | bytes 196612

commit v4 on v3

--- a/solution.py
+++ b/solution.py
@@ -14,7 +14,7 @@
 PLANE = X * Y
 LINE = Z * C
 EARLY = 5
-VMEMLIM = 60
+VMEMLIM = 40
 
 ridge_weight = 0.5
 kernel_gain = 2.0
@@ -51,7 +51,6 @@
 def sweep_inverse(matrix):
     lanes = lax.broadcasted_iota(jnp.int32, (8, R), 1)
     subs = lax.broadcasted_iota(jnp.int32, (8, R), 0)
-    low = lanes < 8
 
     def spread_lane(tile, lane):
         return jnp.broadcast_to(tile[:, lane : lane + 1], (8, R))
@@ -59,11 +58,13 @@
     def spread_line(tile, sub):
         return jnp.broadcast_to(tile[sub : sub + 1, :], (8, R))
 
-    def eight(_, tiles):
-        head = tiles[0]
-        cols = [spread_lane(head, p) for p in range(8)]
+    def eight(block, tiles):
+        start = 8 * block
+        own = (lanes >= start) & (lanes < start + 8)
+        head = tiles[block]
+        cols = [spread_lane(head, start + p) for p in range(8)]
         pivot = {(s, t): spread_line(cols[t], s) for t in range(8) for s in range(t + 1)}
-        rows = [jnp.where(low, jnp.where(lanes == p, -1.0, 0.0), spread_line(head, p)) for p in range(8)]
+        rows = [jnp.where(own, jnp.where(lanes == start + p, -1.0, 0.0), spread_line(head, p)) for p in range(8)]
         for p in range(8):
             inverse = 1.0 / pivot[p, p]
             rows[p] = rows[p] * inverse
@@ -79,24 +80,28 @@
                         pivot[s, t] = pivot[s, t] - pivot[p, s] * ahead[t]
             for t in ahead:
                 pivot[p, t] = ahead[t]
-        turned = []
-        for tile in tiles[1:]:
-            terms = [spread_lane(tile, p) * rows[p] for p in range(8)]
-            while len(terms) > 1:
-                terms = [terms[k] + terms[k + 1] for k in range(0, len(terms), 2)]
-            turned.append(jnp.where(low, 0.0, tile) - terms[0])
         swept = rows[7]
         for p in range(7):
             swept = jnp.where(subs == p, rows[p], swept)
-        turned.append(swept)
-        return tuple(pltpu.roll(tile, R - 8, 1) for tile in turned)
-
-    tiles = tuple(matrix[8 * t : 8 * t + 8, :] for t in range(R // 8))
-    return jnp.concatenate(lax.fori_loop(0, R // 8, eight, tiles, unroll=4), axis=0)
+        after = []
+        for at, tile in enumerate(tiles):
+            if at == block:
+                after.append(swept)
+                continue
+            terms = [spread_lane(tile, start + p) * rows[p] for p in range(8)]
+            while len(terms) > 1:
+                terms = [terms[k] + terms[k + 1] for k in range(0, len(terms), 2)]
+            after.append(jnp.where(own, 0.0, tile) - terms[0])
+        return after
+
+    tiles = [matrix[8 * t : 8 * t + 8, :] for t in range(R // 8)]
+    for block in range(R // 8):
+        tiles = eight(block, tiles)
+    return jnp.concatenate(tiles, axis=0)
 
 
 def kernel(
-    feat_ref, targ_ref, coef_ref, taken_ref, added_ref,
+    feat_ref, targ_ref, coef_ref, resid_ref, change_ref,
     targ_own, block, row_feat, row_targ, row_aug, col_aug, total, outgoing, incoming,
     sq_local, sq_in, sq_sum, sq_line, sq_full,
     cu_local, cu_in, cu_sum, cu_line, cu_full,
@@ -239,7 +244,26 @@
         row_aug[pl.ds(pl.multiple_of(slot * B, B), B), :] = norm_rows(row_feat[slot], True).T.astype(bf16)
         return carry
 
-    lax.fori_loop(1, PLANE // 2, augment, 0)
+
+    def columns(pair):
+        arrived(pair + Z)
+        feats = jnp.concatenate([block[pair, 0:F, :], block[pair + Z, 0:F, :]], axis=1)
+        col_aug[pair] = norm_rows(feats, False).astype(bf16)
+
+    def product(rows, pair):
+        minus = jnp.dot(rows, col_aug[pair], preferred_element_type=f32)
+        entries = jnp.exp2(minus * exponent_scale).astype(bf16)
+        panel = jnp.concatenate([block[pair, F : F + R, :], block[pair + Z, F : F + R, :]], axis=0)
+        return jnp.dot(entries, panel, preferred_element_type=f32)
+
+    def rows_times(first, pairs, fresh):
+        where = pl.ds(first * B, PLANE // 2 * B)
+        rows = row_aug[where, :]
+        value = None if fresh else total[where, :]
+        for pair in pairs:
+            term = product(rows, pair)
+            value = term if value is None else value + term
+        total[where, :] = value
 
     half = (F + R) // 2
     for slot, direction, first in ((2, 1, 0), (Z - 2, Z - 1, half)):
@@ -249,31 +273,19 @@
         rows = pl.ds(first, half)
         send(block.at[slot, rows], block.at[4, rows], line_send.at[1], block_recv.at[4], up(slot))
         across(slot)
+    lax.fori_loop(1, 3, pass_on, 0)
+    lax.fori_loop(1, PLANE // 2, augment, 0)
+    near = (0, 1, Z - 1)
+    for pair in near:
+        columns(pair)
+    rows_times(0, near, True)
     lax.fori_loop(PLANE // 2, PLANE, augment, 0)
-
-    def columns(pair):
-        arrived(pair + Z)
-        feats = jnp.concatenate([block[pair, 0:F, :], block[pair + Z, 0:F, :]], axis=1)
-        col_aug[pair] = norm_rows(feats, False).astype(bf16)
-
-    def product(rows, pair):
-        minus = jnp.dot(rows, col_aug[pair], preferred_element_type=f32)
-        entries = jnp.exp2(minus * exponent_scale).astype(bf16)
-        panel = jnp.concatenate([block[pair, F : F + R, :], block[pair + Z, F : F + R, :]], axis=0)
-        return jnp.dot(entries, panel, preferred_element_type=f32)
-
-    def gathered(step, carry):
-        pair = order(step)
+    lax.fori_loop(EARLY, Z - 1, pass_on, 0)
+    rows_times(PLANE // 2, near, True)
+    lax.fori_loop(Z - 1, Z, pass_on, 0)
+    for pair in (2, Z - 2):
         columns(pair)
         total[...] += product(row_aug[...], pair)
-        return carry
-
-    lax.fori_loop(1, 3, pass_on, 0)
-    columns(0)
-    total[...] = product(row_aug[...], 0)
-    lax.fori_loop(1, EARLY - 1, gathered, 0)
-    lax.fori_loop(EARLY, Z, pass_on, 0)
-    lax.fori_loop(EARLY - 1, EARLY, gathered, 0)
     sum_line(sq_local, sq_in, sq_sum, sq_line, sq_sems)
     last = [(step + 1) // 2 if step % 2 else Z - step // 2 for step in range(EARLY, Z)]
     for pair in last:
@@ -293,15 +305,21 @@
     def finish_rows(step, carry):
         dx = 2 + step - 3 * (step // 2)
         outgoing[pl.ds(dx * Y, Y)] = part(dx).astype(bf16).reshape(Y, B, R)
+
+
+        @pl.when(step < 2)
+        def _():
+            send_group(dx)
+
+        return carry
+
+    def send_group(dx):
         for dy in (2, 1, 3, 0):
             send_rows(dx * Y + dy)
-        return carry
 
     lax.fori_loop(0, X - 1, finish_rows, 0)
     own = part(0)
     outgoing[pl.ds(1, Y - 1)] = own[B:, :].astype(bf16).reshape(Y - 1, B, R)
-    for dy in (2, 1, 3):
-        send_rows(dy)
     own = own[0:B, :]
     row_targs = row_targ.at[pl.ds(1, PLANE - 1)]
     take(row_targs, targ_sems.at[1])
@@ -310,22 +328,24 @@
     term = dot_exact(targ, own) + jnp.dot(targs, images, preferred_element_type=f32)
     cu_local[...] = ridge_weight * sq_local[...] + kernel_gain * term.reshape(PLANE, 8, R)
     reduce_plane(cu_local, cu_in, cu_sems)
-
+    send_group(1)
+    for dy in (2, 1, 3):
+        send_rows(dy)
+
+    sum_line(cu_local, cu_in, cu_sum, cu_line, cu_sems)
     others = incoming.at[pl.ds(1, PLANE - 1)]
     take(others, image_sems.at[1])
 
-    def add(slot, carry):
-        return carry + incoming[slot].astype(f32)
-
-    kernel_image_t = lax.fori_loop(1, PLANE, add, own)
+    kernel_image_t = own
+    for slot in range(1, PLANE):
+        kernel_image_t = kernel_image_t + incoming[slot].astype(f32)
     image_t = ridge_weight * targ_t + kernel_gain * kernel_image_t
     image = image_t.T
     gr_local[...] = dot_exact(image, image_t).reshape(PLANE, 8, R)
     reduce_plane(gr_local, gr_in, gr_sems)
-    sum_line(cu_local, cu_in, cu_sum, cu_line, cu_sems)
     spread_plane(sq_sum, sq_line, sq_full, sq_sems)
+    spread_plane(cu_sum, cu_line, cu_full, cu_sems)
     sum_line(gr_local, gr_in, gr_sum, gr_line, gr_sems)
-    spread_plane(cu_sum, cu_line, cu_full, cu_sems)
     spread_plane(gr_sum, gr_line, gr_full, gr_sems)
 
     finish(cu_in, cu_sems)
@@ -337,12 +357,13 @@
     step_size = -dot_exact(minus_inverse, squares)
     step_t = step_size.T
     coef_ref[...] = dot_exact(step_t, targ)
-    taken_ref[...] = dot_exact(step_t, image)
+    residual = targ - dot_exact(step_t, image)
+    resid_ref[...] = residual
     solved = dot_exact(minus_inverse, targ)
     before = dot_exact(curvature, solved)
     finish(gr_in, gr_sems)
     image_gram = gr_full[...].reshape(R, R)
-    added_ref[...] = before - dot_exact(step_t, dot_exact(image_gram, solved))
+    change_ref[...] = before - dot_exact(step_t, dot_exact(image_gram, solved))
 
     take(row_feat.at[pl.ds(1, PLANE - 1)], row_send.at[0])
     take(row_targs, targ_sems.at[0])
@@ -354,6 +375,13 @@
     take(block.at[pl.ds(1, 3)], line_send.at[1])
     for slot in range(Z):
         take(block.at[slot], cross_send.at[slot])
+
+
+def place(coef_ref, resid_ref, change_ref, coef_out, resid_out, dir_out):
+    coef_out[...] = coef_ref[...]
+    residual = resid_ref[...]
+    resid_out[...] = residual
+    dir_out[...] = residual + change_ref[...]
 
 
 def local(features, targets):
@@ -368,7 +396,7 @@
         pltpu.VMEM((LINE - 1, 8, R), f32),
         pltpu.VMEM((PLANE, 8, R), f32),
     ]
-    coefficients, taken, added = pl.pallas_call(
+    results = pl.pallas_call(
         kernel,
         out_shape=(whole, whole, whole),
         in_specs=[hbm, hbm],
@@ -400,8 +428,13 @@
             collective_id=0, has_side_effects=True, vmem_limit_bytes=VMEMLIM * 1024 * 1024
         ),
     )(features, targets)
-    residual = targets - taken
-    return coefficients, residual, residual + added
+    return pl.pallas_call(
+        place,
+        out_shape=(whole, whole, whole),
+        in_specs=[vmem] * 3,
+        out_specs=(vmem, vmem, vmem),
+        compiler_params=pltpu.CompilerParams(vmem_limit_bytes=2 * 1024 * 1024),
+    )(*results)
 
 
 def solution(mesh):

time: 57 us -> 54.4 us (0.954)
  Pallas kernels: 54 us -> 52 us
  other arithmetic: 1.56 us -> 0 us
  local copies, waits for them, and re-layouts: 0.64 us -> 1.55 us
    pallas_call x1, Pallas kernels: 54 us -> 51.3 us  [local(): pl.pallas_call(kernel, out_shape=(whole, whole, whole), in_specs=[hbm, hb...]
    add x1 -> x0, other arithmetic: 1.56 us -> none  [local(): return (coefficients, residual, residual + added)]
    unnamed x5 -> x4, local copies, waits for them, and re-layouts: 0.64 us -> 1.55 us
    pallas_call x0 -> x1, Pallas kernels: none -> 0.69 us  [local(): pl.pallas_call(place, out_shape=(whole, whole, whole), in_specs=[vmem] *...]
where the time goes in v4:
time: 54.4 us; the launch traced here: 54.2 us
  Pallas kernels  52 us (96%)
  local copies, waits for them, and re-layouts  1.55 us (3%)
  between operations  0.65 us (1%)
    pallas_call x1, Pallas kernels, local(): pl.pallas_call(kernel, out_shape=(whole, whole, whole), in_specs=[hbm, hb...  51.3 us
    unnamed x4, local copies, waits for them, and re-layouts  1.55 us

profile of v4, /device:TPU:1, one launch (start us, length us, event | category | flops | bytes accessed | tf_op | source)
XLA Modules:
  0.0 54.2 jit_solution(12649023780829470310)
XLA Ops:
  0.6 0.0 copy-start
  0.6 0.8 %copy-done = f32[128,128]{1,0:T(8,128)S(1)} copy-done((f32[128,128]{1,0:T(8,128)S(1)}, f32[128,128]{1,0:T(8,128)}, u32[]{:S(2)}) %copy-start) | copy-done | bytes 65560
  1.5 0.0 copy-start.1
  1.5 0.7 %copy-done.1 = bf16[64,128]{1,0:T(8,128)(2,1)S(1)} copy-done((bf16[64,128]{1,0:T(8,128)(2,1)S(1)}, bf16[64,128]{1,0:T(8,128)(2,1)}, u32[]{:S(2)}) %copy-start.1) | copy-done | bytes 16408
  2.2 51.3 %shard_map.49 = (f32[128,128]{1,0:T(8,128)S(1)}, f32[128,128]{1,0:T(8,128)S(1)}, f32[128,128]{1,0:T(8,128)S(1)}) custom-call(bf16[64,128]{1,0:T(8,128)(2,1)S(1)} %copy-done.1, f32[128,128]{1,0:T(8,128)S(1)} %copy-done), custom_call_target="tpu_custom_call" | custom-call | tf_op jit(solution)/shard_map/pallas_call | solution.py:399
  53.5 0.7 %shard_map.50 = (f32[128,128]{1,0:T(8,128)}, f32[128,128]{1,0:T(8,128)}, f32[128,128]{1,0:T(8,128)}) custom-call(f32[128,128]{1,0:T(8,128)S(1)} %get-tuple-element.6.coef_ref, f32[128,128]{1,0:T(8,128)S(1)} %get-tuple-element.7.resid_ref, f32[128,128]{1,0:T(8,128)S(1)} %get-tuple-element.8.change_ref), custom_call_target="tpu_custom_call" | custom-call | tf_op jit(solution)/shard_map/pallas_call | solution.py:431
Async XLA Ops:
  0.6 0.8 %copy-start = (f32[128,128]{1,0:T(8,128)S(1)}, f32[128,128]{1,0:T(8,128)}, u32[]{:S(2)}) copy-start(f32[128,128]{1,0:T(8,128)} %targ_ref.1) | copy-start | bytes 196612
  1.5 0.7 %copy-start.1 = (bf16[64,128]{1,0:T(8,128)(2,1)S(1)}, bf16[64,128]{1,0:T(8,128)(2,1)}, u32[]{:S(2)}) copy-start(bf16[64,128]{1,0:T(8,128)(2,1)} %feat_ref.1) | copy-start | bytes 49156

commit v5 on v4

--- a/solution.py
+++ b/solution.py
@@ -102,11 +102,11 @@
 
 def kernel(
     feat_ref, targ_ref, coef_ref, resid_ref, change_ref,
-    targ_own, block, row_feat, row_targ, row_aug, col_aug, total, outgoing, incoming,
+    block, row_feat, row_targ, row_aug, col_aug, total, outgoing, incoming,
     sq_local, sq_in, sq_sum, sq_line, sq_full,
     cu_local, cu_in, cu_sum, cu_line, cu_full,
     gr_local, gr_in, gr_sum, gr_line, gr_full,
-    load_sems, block_recv, cross_send, line_send, row_recv, row_send, targ_sems, image_sems, sq_sems, cu_sems, gr_sems,
+    block_recv, cross_send, line_send, row_recv, row_send, targ_sems, image_sems, sq_sems, cu_sems, gr_sems,
 ):
     row, col = lax.axis_index("row"), lax.axis_index("col")
     x, z = row // Z, row % Z
@@ -148,13 +148,8 @@
 
     lax.fori_loop(1, PLANE, greet, 0)
 
-    load_feat = pltpu.make_async_copy(feat_ref, block.at[0, pl.ds(0, F)], load_sems.at[0])
-    load_targ = pltpu.make_async_copy(targ_ref, targ_own, load_sems.at[1])
-    load_targ.start()
-    load_feat.start()
-    load_targ.wait()
-    load_feat.wait()
-    targ = targ_own[...]
+    block[0, 0:F, :] = feat_ref[...]
+    targ = targ_ref[...]
     targ_t = targ.T
     targ_high = targ.astype(bf16)
     row_targ[0] = targ_high
@@ -291,8 +286,8 @@
     for pair in last:
         columns(pair)
 
-    def part(dx):
-        where = pl.ds(pl.multiple_of(dx * Y * B, Y * B), Y * B)
+    def part(first):
+        where = pl.ds(first * B, PLANE // 2 * B)
         rows = row_aug[where, :]
         value = total[where, :]
         for pair in last:
@@ -302,24 +297,15 @@
     def send_rows(slot):
         send(outgoing.at[slot], incoming.at[slot], image_sems.at[0], image_sems.at[1], at_plane_back(slot))
 
-    def finish_rows(step, carry):
-        dx = 2 + step - 3 * (step // 2)
-        outgoing[pl.ds(dx * Y, Y)] = part(dx).astype(bf16).reshape(Y, B, R)
-
-
-        @pl.when(step < 2)
-        def _():
-            send_group(dx)
-
-        return carry
-
     def send_group(dx):
         for dy in (2, 1, 3, 0):
             send_rows(dx * Y + dy)
 
-    lax.fori_loop(0, X - 1, finish_rows, 0)
+    outgoing[PLANE // 2 :] = part(PLANE // 2).astype(bf16).reshape(PLANE // 2, B, R)
+    send_group(2)
+    send_group(3)
     own = part(0)
-    outgoing[pl.ds(1, Y - 1)] = own[B:, :].astype(bf16).reshape(Y - 1, B, R)
+    outgoing[1 : PLANE // 2] = own[B:, :].astype(bf16).reshape(PLANE // 2 - 1, B, R)
     own = own[0:B, :]
     row_targs = row_targ.at[pl.ds(1, PLANE - 1)]
     take(row_targs, targ_sems.at[1])
@@ -387,7 +373,6 @@
 def local(features, targets):
     whole = jax.ShapeDtypeStruct((R, B), f32)
     vmem = pl.BlockSpec(memory_space=pltpu.VMEM)
-    hbm = pl.BlockSpec(memory_space=pltpu.HBM)
     dma = pltpu.SemaphoreType.DMA
     sums = [
         pltpu.VMEM((PLANE, 8, R), f32),
@@ -399,10 +384,9 @@
     results = pl.pallas_call(
         kernel,
         out_shape=(whole, whole, whole),
-        in_specs=[hbm, hbm],
+        in_specs=[vmem, vmem],
         out_specs=(vmem, vmem, vmem),
         scratch_shapes=[
-            pltpu.VMEM((R, B), f32),
             pltpu.VMEM((LINE, F + R, B), bf16),
             pltpu.VMEM((PLANE, F, B), bf16),
             pltpu.VMEM((PLANE, R, B), bf16),
@@ -412,7 +396,6 @@
             pltpu.VMEM((PLANE, B, R), bf16),
             pltpu.VMEM((PLANE, B, R), bf16),
             *sums, *sums, *sums,
-            dma((2,)),
             dma((LINE,)),
             dma((Z,)),
             dma((2,)),

time: 54.4 us -> 54.4 us (level)
  no operation moved by 1% of the time
where the time goes in v5:
time: 54.4 us; the launch traced here: 54.3 us
  Pallas kernels  52.1 us (96%)
  local copies, waits for them, and re-layouts  1.55 us (3%)
  between operations  0.65 us (1%)
    pallas_call x1, Pallas kernels, local(): pl.pallas_call(kernel, out_shape=(whole, whole, whole), in_specs=[vmem, v...  51.4 us
    unnamed x4, local copies, waits for them, and re-layouts  1.55 us

profile of v5, /device:TPU:1, one launch (start us, length us, event | category | flops | bytes accessed | tf_op | source)
XLA Modules:
  0.0 54.3 jit_solution(6831661399476243372)
XLA Ops:
  0.6 0.0 copy-start
  0.6 0.8 %copy-done = f32[128,128]{1,0:T(8,128)S(1)} copy-done((f32[128,128]{1,0:T(8,128)S(1)}, f32[128,128]{1,0:T(8,128)}, u32[]{:S(2)}) %copy-start) | copy-done | bytes 65560
  1.5 0.0 copy-start.1
  1.5 0.7 %copy-done.1 = bf16[64,128]{1,0:T(8,128)(2,1)S(1)} copy-done((bf16[64,128]{1,0:T(8,128)(2,1)S(1)}, bf16[64,128]{1,0:T(8,128)(2,1)}, u32[]{:S(2)}) %copy-start.1) | copy-done | bytes 16408
  2.2 51.4 %shard_map.49 = (f32[128,128]{1,0:T(8,128)S(1)}, f32[128,128]{1,0:T(8,128)S(1)}, f32[128,128]{1,0:T(8,128)S(1)}) custom-call(bf16[64,128]{1,0:T(8,128)(2,1)S(1)} %copy-done.1, f32[128,128]{1,0:T(8,128)S(1)} %copy-done), custom_call_target="tpu_custom_call" | custom-call | tf_op jit(solution)/shard_map/pallas_call | solution.py:384
  53.6 0.7 %shard_map.50 = (f32[128,128]{1,0:T(8,128)}, f32[128,128]{1,0:T(8,128)}, f32[128,128]{1,0:T(8,128)}) custom-call(f32[128,128]{1,0:T(8,128)S(1)} %get-tuple-element.6.coef_ref, f32[128,128]{1,0:T(8,128)S(1)} %get-tuple-element.7.resid_ref, f32[128,128]{1,0:T(8,128)S(1)} %get-tuple-element.8.change_ref), custom_call_target="tpu_custom_call" | custom-call | tf_op jit(solution)/shard_map/pallas_call | solution.py:414
Async XLA Ops:
  0.6 0.8 %copy-start = (f32[128,128]{1,0:T(8,128)S(1)}, f32[128,128]{1,0:T(8,128)}, u32[]{:S(2)}) copy-start(f32[128,128]{1,0:T(8,128)} %targ_ref.1) | copy-start | bytes 196612
  1.5 0.7 %copy-start.1 = (bf16[64,128]{1,0:T(8,128)(2,1)S(1)}, bf16[64,128]{1,0:T(8,128)(2,1)}, u32[]{:S(2)}) copy-start(bf16[64,128]{1,0:T(8,128)(2,1)} %feat_ref.1) | copy-start | bytes 49156

commit v6 on v5

--- a/solution.py
+++ b/solution.py
@@ -222,7 +222,7 @@
     sq_local[...] = dot_exact(targ, targ_t).reshape(PLANE, 8, R)
     reduce_plane(sq_local, sq_in, sq_sems)
     lax.fori_loop(1, PLANE, send_targ, 0)
-    row_aug[0:B, :] = norm_rows(block[0, 0:F, :], True).T.astype(bf16)
+    row_aug[0:B, :] = norm_rows(block[0, 0:F, :], True).astype(bf16).T
 
     def arrived(slot):
         take(block.at[slot], block_recv.at[slot])
@@ -236,7 +236,7 @@
     def augment(step, carry):
         slot = plane_order(step)
         take(row_feat.at[slot], row_recv.at[slot])
-        row_aug[pl.ds(pl.multiple_of(slot * B, B), B), :] = norm_rows(row_feat[slot], True).T.astype(bf16)
+        row_aug[pl.ds(pl.multiple_of(slot * B, B), B), :] = norm_rows(row_feat[slot], True).astype(bf16).T
         return carry
 
 

time: 54.4 us -> 54.3 us (level)
  no operation moved by 1% of the time
where the time goes in v6:
time: 54.3 us; the launch traced here: 54.1 us
  Pallas kernels  51.9 us (96%)
  local copies, waits for them, and re-layouts  1.55 us (3%)
  between operations  0.65 us (1%)
    pallas_call x1, Pallas kernels, local(): pl.pallas_call(kernel, out_shape=(whole, whole, whole), in_specs=[vmem, v...  51.2 us
    unnamed x4, local copies, waits for them, and re-layouts  1.55 us

profile of v6, /device:TPU:1, one launch (start us, length us, event | category | flops | bytes accessed | tf_op | source)
XLA Modules:
  0.0 54.1 jit_solution(17482351596763042618)
XLA Ops:
  0.6 0.0 copy-start
  0.6 0.8 %copy-done = f32[128,128]{1,0:T(8,128)S(1)} copy-done((f32[128,128]{1,0:T(8,128)S(1)}, f32[128,128]{1,0:T(8,128)}, u32[]{:S(2)}) %copy-start) | copy-done | bytes 65560
  1.5 0.0 copy-start.1
  1.5 0.7 %copy-done.1 = bf16[64,128]{1,0:T(8,128)(2,1)S(1)} copy-done((bf16[64,128]{1,0:T(8,128)(2,1)S(1)}, bf16[64,128]{1,0:T(8,128)(2,1)}, u32[]{:S(2)}) %copy-start.1) | copy-done | bytes 16408
  2.2 51.2 %shard_map.49 = (f32[128,128]{1,0:T(8,128)S(1)}, f32[128,128]{1,0:T(8,128)S(1)}, f32[128,128]{1,0:T(8,128)S(1)}) custom-call(bf16[64,128]{1,0:T(8,128)(2,1)S(1)} %copy-done.1, f32[128,128]{1,0:T(8,128)S(1)} %copy-done), custom_call_target="tpu_custom_call" | custom-call | tf_op jit(solution)/shard_map/pallas_call | solution.py:384
  53.4 0.7 %shard_map.50 = (f32[128,128]{1,0:T(8,128)}, f32[128,128]{1,0:T(8,128)}, f32[128,128]{1,0:T(8,128)}) custom-call(f32[128,128]{1,0:T(8,128)S(1)} %get-tuple-element.6.coef_ref, f32[128,128]{1,0:T(8,128)S(1)} %get-tuple-element.7.resid_ref, f32[128,128]{1,0:T(8,128)S(1)} %get-tuple-element.8.change_ref), custom_call_target="tpu_custom_call" | custom-call | tf_op jit(solution)/shard_map/pallas_call | solution.py:414
Async XLA Ops:
  0.6 0.8 %copy-start = (f32[128,128]{1,0:T(8,128)S(1)}, f32[128,128]{1,0:T(8,128)}, u32[]{:S(2)}) copy-start(f32[128,128]{1,0:T(8,128)} %targ_ref.1) | copy-start | bytes 196612
  1.5 0.7 %copy-start.1 = (bf16[64,128]{1,0:T(8,128)(2,1)S(1)}, bf16[64,128]{1,0:T(8,128)(2,1)}, u32[]{:S(2)}) copy-start(bf16[64,128]{1,0:T(8,128)(2,1)} %feat_ref.1) | copy-start | bytes 49156
